TPU v7x, 512 devices: a whole 4x4x16 slice. The times are simulated.
512 devices in a mesh: ctx: 64 (over y, z_lo, core), ch: 8 (over z_hi, x).
Axes of the slice: x: 4, y: 4, z: 16 (z_hi: 2, z_lo: 8; z = z_hi * 8 + z_lo), core: 2. Of those that a mesh axis runs over, the one named last changes fastest.
Arguments:
- x_one: bfloat16 [8192, 4096], P('ctx', 'ch'), may hold values from -6 to 6
- x_two: bfloat16 [8192, 4096], P('ctx', 'ch'), may hold values from -6 to 6
- values: bfloat16 [8192, 4096], P('ctx', 'ch'), may hold values from -6 to 6
- grad_out: bfloat16 [8192, 4096], P('ctx', 'ch'), may hold values from -3 to 3
- filter_raw: bfloat16 [1024, 512], P('ctx', 'ch'), may hold values from -4 to 4
Outputs:
- grad_x_one: bfloat16 [8192, 4096], P('ctx', 'ch')
- grad_x_two: bfloat16 [8192, 4096], P('ctx', 'ch')
- grad_values: bfloat16 [8192, 4096], P('ctx', 'ch')
- grad_filter: float32 [1024, 512], P('ctx', 'ch')
All inputs are finite; a program needn't handle non-finite values.
Results may differ from a plain program's by a relative error of at most 0.0049.
Values may be sent and summed in bfloat16 or wider, within the bound.
A program may use at most 64 MiB of HBM per device.

v0:
```python
import math
import jax
import jax.numpy as jnp
from jax import lax
from jax.sharding import PartitionSpec as P

highest = lax.Precision.HIGHEST


def shifted(value, axis, by):
    peers = lax.axis_size(axis)
    pairs = [(i, i + by) for i in range(peers) if 0 <= i + by < peers]
    return lax.ppermute(value, axis, pairs)


def dft_tables(tok):
    size = 2 * tok
    freq = jnp.arange(tok + 1, dtype=jnp.int32)
    place = jnp.arange(tok, dtype=jnp.int32)

    def angles(rows, cols):
        return 2.0 * math.pi / size * (rows[:, None] * cols[None, :] % size).astype(jnp.float32)

    forward_angle = angles(freq, place)
    forward_table = jnp.concatenate([jnp.cos(forward_angle), -jnp.sin(forward_angle)], axis=0)
    weights = jnp.where((freq == 0) | (freq == tok), 1.0, 2.0).astype(jnp.float32) / size

    def inverse(points):
        angle = angles(points, freq)
        return jnp.concatenate(
            [weights[None, :] * jnp.cos(angle), -weights[None, :] * jnp.sin(angle)], axis=1
        )

    lower_table = inverse(place)
    upper_table = inverse(place + tok)
    lag_table = inverse(tok - place)
    signs = (1 - 2 * (freq % 2)).astype(jnp.float32)
    return (forward_table, lower_table, upper_table, lag_table, signs)


def weigh_plain(fil_real, fil_imag, spec_real, spec_imag):
    real = jnp.sum(fil_real * spec_real - fil_imag * spec_imag, axis=0)
    imag = jnp.sum(fil_real * spec_imag + fil_imag * spec_real, axis=0)
    return (real, imag)


def weigh_conj(fil_real, fil_imag, spec_real, spec_imag):
    real = jnp.sum(fil_real * spec_real + fil_imag * spec_imag, axis=0)
    imag = jnp.sum(fil_real * spec_imag - fil_imag * spec_real, axis=0)
    return (real, imag)


def local(x_one, x_two, values, grad_out, filter_raw):
    tok, chans = x_one.shape
    piece = lax.all_gather(filter_raw, "ctx", axis=0, tiled=True)
    whole = lax.all_gather(piece, "ch", axis=1, tiled=True)
    taps, groups = whole.shape
    span = taps // tok
    repeat = chans // groups
    bins = tok + 1
    scale = 1.0 / math.sqrt(taps)
    forward_table, lower_table, upper_table, lag_table, signs = dft_tables(tok)
    filt = whole.astype(jnp.float32) * scale
    filt_spec = jnp.einsum(
        "mt,ktf->kmf", forward_table, filt.reshape(span, tok, groups), precision=highest
    )
    filt_real = filt_spec[:, :bins, :][:, :, None, :]
    filt_imag = filt_spec[:, bins:, :][:, :, None, :]
    product_in = (x_one.astype(jnp.float32) * values.astype(jnp.float32)).astype(jnp.bfloat16)
    grad_conv = (grad_out.astype(jnp.float32) * x_two.astype(jnp.float32)).astype(jnp.bfloat16)
    lower_list = [product_in]
    upper_list = [grad_conv]
    lower_block = product_in
    upper_block = grad_conv
    for offset in range(1, span + 1):
        lower_block = shifted(lower_block, "ctx", 1)
        upper_block = shifted(upper_block, "ctx", -1)
        lower_list.append(lower_block)
        upper_list.append(upper_block)

    def spectra(blocks):
        stacked = jnp.stack(blocks).astype(jnp.float32)
        spec = jnp.einsum("mt,ktc->kmc", forward_table, stacked, precision=highest)
        return (
            spec[:, :bins].reshape(span + 1, bins, repeat, groups),
            spec[:, bins:].reshape(span + 1, bins, repeat, groups),
        )

    in_real, in_imag = spectra(lower_list)
    grad_real, grad_imag = spectra(upper_list)
    forward_lo = weigh_plain(filt_real, filt_imag, in_real[:span], in_imag[:span])
    forward_hi = weigh_plain(filt_real, filt_imag, in_real[1:], in_imag[1:])
    backward_lo = weigh_conj(filt_real, filt_imag, grad_real[:span], grad_imag[:span])
    backward_hi = weigh_conj(filt_real, filt_imag, grad_real[1:], grad_imag[1:])
    own_real = grad_real[0]
    own_imag = grad_imag[0]
    cross_real = jnp.sum(own_real * in_real + own_imag * in_imag, axis=2)
    cross_imag = jnp.sum(own_real * in_imag - own_imag * in_real, axis=2)

    def inverse_apply(table, parts):
        stacked = jnp.concatenate([parts[0], parts[1]], axis=0).reshape(2 * bins, chans)
        return jnp.dot(table, stacked, precision=highest)

    conv_out = inverse_apply(lower_table, forward_lo) + inverse_apply(upper_table, forward_hi)
    grad_in = inverse_apply(lower_table, backward_lo) + inverse_apply(upper_table, backward_hi)
    grad_x_one = (grad_in * values.astype(jnp.float32)).astype(jnp.bfloat16)
    grad_x_two = (grad_out.astype(jnp.float32) * conv_out).astype(jnp.bfloat16)
    grad_values = (grad_in * x_one.astype(jnp.float32)).astype(jnp.bfloat16)
    lag_real = cross_real[1:] + signs[None, :, None] * cross_real[:-1]
    lag_imag = cross_imag[1:] + signs[None, :, None] * cross_imag[:-1]
    lag_spec = jnp.concatenate([lag_real, lag_imag], axis=1)
    filter_terms = (
        jnp.einsum("rm,kmf->krf", lag_table, lag_spec, precision=highest).reshape(taps, groups)
        * scale
    )
    by_taps = lax.psum_scatter(filter_terms, "ctx", scatter_dimension=0, tiled=True)
    grad_filter = lax.psum_scatter(by_taps, "ch", scatter_dimension=1, tiled=True)
    return (grad_x_one, grad_x_two, grad_values, grad_filter)


def solution(mesh):
    placed = (P("ctx", "ch"), P("ctx", "ch"), P("ctx", "ch"), P("ctx", "ch"), P("ctx", "ch"))
    return jax.shard_map(
        local,
        mesh=mesh,
        in_specs=placed,
        out_specs=(P("ctx", "ch"), P("ctx", "ch"), P("ctx", "ch"), P("ctx", "ch")),
        check_vma=False,
    )
```

profile of v0, /device:TPU:8, one launch (start us, length us, event | category | flops | bytes accessed | tf_op | source)
XLA Modules:
  0.0 816.9 jit_solution(427479515096620973)
XLA Ops:
  9.0 1.9 collective-permute-start.8
  11.0 114.9 %all_gather.6 = bf16[1024,64]{1,0:T(8,128)(2,1)S(1)} all-gather(bf16[16,64]{1,0:T(8,128)(2,1)} %param.9), channel_id=1, replica_groups=mesh['ctx'=64,'ch'=8] {'ctx'}, dimensions={0}, use_global_device_ids=true | all-gather | bytes 133120 | tf_op jit(solution)/shard_map/all_gather | solution.py:55
  127.7 1.9 collective-permute-start
  131.5 2.4 collective-permute-start.9
  133.9 10.7 %collective-permute-start.1 = (bf16[128,512]{1,0:T(8,128)(2,1)S(1)}, bf16[128,512]{1,0:T(8,128)(2,1)S(1)}, u32[]{:S(2)}, u32[]{:S(2)}) collective-permute-start(bf16[128,512]{1,0:T(8,128)(2,1)S(1)} %collective-permute-done), channel_id=1, source_target_pairs={{8,0},{16,8},{24,16},{32,24},{40,32},{48,40},{56,48},{64,56},{72,6... | collective-permute-start | bytes 393224 | tf_op jit(solution)/shard_map/ppermute | solution.py:13
  147.3 11.3 %collective-permute-start.2 = (bf16[128,512]{1,0:T(8,128)(2,1)S(1)}, bf16[128,512]{1,0:T(8,128)(2,1)S(1)}, u32[]{:S(2)}, u32[]{:S(2)}) collective-permute-start(bf16[128,512]{1,0:T(8,128)(2,1)S(1)} %collective-permute-done.1), channel_id=1, source_target_pairs={{8,0},{16,8},{24,16},{32,24},{40,32},{48,40},{56,48},{64,56},{72,6... | collective-permute-start | bytes 393224 | tf_op jit(solution)/shard_map/ppermute | solution.py:13
  162.4 11.3 %collective-permute-start.3 = (bf16[128,512]{1,0:T(8,128)(2,1)S(1)}, bf16[128,512]{1,0:T(8,128)(2,1)S(1)}, u32[]{:S(2)}, u32[]{:S(2)}) collective-permute-start(bf16[128,512]{1,0:T(8,128)(2,1)S(1)} %collective-permute-done.2), channel_id=1, source_target_pairs={{8,0},{16,8},{24,16},{32,24},{40,32},{48,40},{56,48},{64,56},{72,6... | collective-permute-start | bytes 393224 | tf_op jit(solution)/shard_map/ppermute | solution.py:13
  173.8 1.9 collective-permute-start.12
  176.2 11.4 %collective-permute-start.4 = (bf16[128,512]{1,0:T(8,128)(2,1)S(1)}, bf16[128,512]{1,0:T(8,128)(2,1)S(1)}, u32[]{:S(2)}, u32[]{:S(2)}) collective-permute-start(bf16[128,512]{1,0:T(8,128)(2,1)S(1)} %collective-permute-done.3), channel_id=1, source_target_pairs={{8,0},{16,8},{24,16},{32,24},{40,32},{48,40},{56,48},{64,56},{72,6... | collective-permute-start | bytes 393224 | tf_op jit(solution)/shard_map/ppermute | solution.py:13
  189.7 8.4 %collective-permute-done.4 = bf16[128,512]{1,0:T(8,128)(2,1)S(1)} collective-permute-done((bf16[128,512]{1,0:T(8,128)(2,1)S(1)}, bf16[128,512]{1,0:T(8,128)(2,1)S(1)}, u32[]{:S(2)}, u32[]{:S(2)}) %collective-permute-start.4) | collective-permute-done | bytes 131104 | tf_op jit(solution)/shard_map/ppermute | solution.py:13
  198.1 11.7 %collective-permute-start.5 = (bf16[128,512]{1,0:T(8,128)(2,1)S(1)}, bf16[128,512]{1,0:T(8,128)(2,1)S(1)}, u32[]{:S(2)}, u32[]{:S(2)}) collective-permute-start(bf16[128,512]{1,0:T(8,128)(2,1)S(1)} %collective-permute-done.4), channel_id=1, source_target_pairs={{8,0},{16,8},{24,16},{32,24},{40,32},{48,40},{56,48},{64,56},{72,6... | collective-permute-start | bytes 393224 | tf_op jit(solution)/shard_map/ppermute | solution.py:13
  209.8 4.0 collective-permute-done.13
  215.7 11.1 %collective-permute-start.6 = (bf16[128,512]{1,0:T(8,128)(2,1)S(1)}, bf16[128,512]{1,0:T(8,128)(2,1)S(1)}, u32[]{:S(2)}, u32[]{:S(2)}) collective-permute-start(bf16[128,512]{1,0:T(8,128)(2,1)S(1)} %collective-permute-done.5), channel_id=1, source_target_pairs={{8,0},{16,8},{24,16},{32,24},{40,32},{48,40},{56,48},{64,56},{72,6... | collective-permute-start | bytes 393224 | tf_op jit(solution)/shard_map/ppermute | solution.py:13
  229.5 11.3 %collective-permute-start.7 = (bf16[128,512]{1,0:T(8,128)(2,1)S(1)}, bf16[128,512]{1,0:T(8,128)(2,1)S(1)}, u32[]{:S(2)}, u32[]{:S(2)}) collective-permute-start(bf16[128,512]{1,0:T(8,128)(2,1)S(1)} %collective-permute-done.6), channel_id=1, source_target_pairs={{8,0},{16,8},{24,16},{32,24},{40,32},{48,40},{56,48},{64,56},{72,6... | collective-permute-start | bytes 393224 | tf_op jit(solution)/shard_map/ppermute | solution.py:13
  240.9 2.3 collective-permute-done.7
  243.2 2.3 convolution_bitcast_fusion.1
  245.6 2.4 convolution_bitcast_fusion
  251.0 7.3 fusion.6
  258.6 2.9 convert_multiply_fusion
  261.5 1.9 copy.12
  263.5 4.1 convolution_bitcast_fusion.2
  267.6 8.1 subtract_reduce_fusion
  278.5 388.4 %reduce-scatter.5.cloned.1.call-done = f32[16,512]{1,0:T(8,128)} async-done(((f32[1024,512]{1,0:T(8,128)}), f32[16,512]{1,0:T(8,128)}) %reduce-scatter.5.cloned.1.call-update) | async-done | bytes 32784 | tf_op jit(solution)/shard_map/reduce_scatter | solution.py:116
  669.8 138.2 %reduce-scatter.7.cloned.1.call-done = f32[64,16]{1,0:T(8,128)} async-done(((f32[512,16]{1,0:T(8,128)}), f32[64,16]{1,0:T(8,128)}) %reduce-scatter.7.cloned.1.call-update) | async-done | bytes 4112
  (72 shorter events, 28.8 us)
Async XLA Ops:
  8.0 250.6 %all-gather.2.cloned.1.call-start = ((), (), s32[]{:S(2)}) async-start(), calls=%async_computation.2 | async-start | bytes 1179648 | tf_op jit(solution)/shard_map/all_gather | solution.py:56
  9.0 122.4 %collective-permute-start.8 = (bf16[128,512]{1,0:T(8,128)(2,1)S(1)}, bf16[128,512]{1,0:T(8,128)(2,1)S(1)}, u32[]{:S(2)}, u32[]{:S(2)}) collective-permute-start(bf16[128,512]{1,0:T(8,128)(2,1)S(1)} %get-tuple-element.13), channel_id=1, source_target_pairs={{0,8},{8,16},{16,24},{24,32},{32,40},{40,48},{48,56},{56,64},{64,7... | collective-permute-start | bytes 393224 | tf_op jit(solution)/shard_map/ppermute | solution.py:13
  126.7 540.2 %reduce-scatter.5.cloned.1.call-start = ((), (), s32[]{:S(2)}) async-start(), calls=%async_computation.3 | async-start | bytes 2129920 | tf_op jit(solution)/shard_map/reduce_scatter | solution.py:116
  127.7 6.2 collective-permute-start
  131.5 13.9 %collective-permute-start.9 = (bf16[128,512]{1,0:T(8,128)(2,1)S(1)}, bf16[128,512]{1,0:T(8,128)(2,1)S(1)}, u32[]{:S(2)}, u32[]{:S(2)}) collective-permute-start(bf16[128,512]{1,0:T(8,128)(2,1)S(1)} %collective-permute-done.8), channel_id=1, source_target_pairs={{0,8},{8,16},{16,24},{24,32},{32,40},{40,48},{48,56},{56,64},{64,7... | collective-permute-start | bytes 393224 | tf_op jit(solution)/shard_map/ppermute | solution.py:13
  133.9 13.4 %collective-permute-start.1 = (bf16[128,512]{1,0:T(8,128)(2,1)S(1)}, bf16[128,512]{1,0:T(8,128)(2,1)S(1)}, u32[]{:S(2)}, u32[]{:S(2)}) collective-permute-start(bf16[128,512]{1,0:T(8,128)(2,1)S(1)} %collective-permute-done), channel_id=1, source_target_pairs={{8,0},{16,8},{24,16},{32,24},{40,32},{48,40},{56,48},{64,56},{72,6... | collective-permute-start | bytes 393224 | tf_op jit(solution)/shard_map/ppermute | solution.py:13
  145.4 14.1 %collective-permute-start.10 = (bf16[128,512]{1,0:T(8,128)(2,1)S(1)}, bf16[128,512]{1,0:T(8,128)(2,1)S(1)}, u32[]{:S(2)}, u32[]{:S(2)}) collective-permute-start(bf16[128,512]{1,0:T(8,128)(2,1)S(1)} %collective-permute-done.9), channel_id=1, source_target_pairs={{0,8},{8,16},{16,24},{24,32},{32,40},{40,48},{48,56},{56,64},{64,7... | collective-permute-start | bytes 393224 | tf_op jit(solution)/shard_map/ppermute | solution.py:13
  147.3 15.1 %collective-permute-start.2 = (bf16[128,512]{1,0:T(8,128)(2,1)S(1)}, bf16[128,512]{1,0:T(8,128)(2,1)S(1)}, u32[]{:S(2)}, u32[]{:S(2)}) collective-permute-start(bf16[128,512]{1,0:T(8,128)(2,1)S(1)} %collective-permute-done.1), channel_id=1, source_target_pairs={{8,0},{16,8},{24,16},{32,24},{40,32},{48,40},{56,48},{64,56},{72,6... | collective-permute-start | bytes 393224 | tf_op jit(solution)/shard_map/ppermute | solution.py:13
  159.4 14.3 %collective-permute-start.11 = (bf16[128,512]{1,0:T(8,128)(2,1)S(1)}, bf16[128,512]{1,0:T(8,128)(2,1)S(1)}, u32[]{:S(2)}, u32[]{:S(2)}) collective-permute-start(bf16[128,512]{1,0:T(8,128)(2,1)S(1)} %collective-permute-done.10), channel_id=1, source_target_pairs={{0,8},{8,16},{16,24},{24,32},{32,40},{40,48},{48,56},{56,64},{64,7... | collective-permute-start | bytes 393224 | tf_op jit(solution)/shard_map/ppermute | solution.py:13
  162.4 13.8 %collective-permute-start.3 = (bf16[128,512]{1,0:T(8,128)(2,1)S(1)}, bf16[128,512]{1,0:T(8,128)(2,1)S(1)}, u32[]{:S(2)}, u32[]{:S(2)}) collective-permute-start(bf16[128,512]{1,0:T(8,128)(2,1)S(1)} %collective-permute-done.2), channel_id=1, source_target_pairs={{8,0},{16,8},{24,16},{32,24},{40,32},{48,40},{56,48},{64,56},{72,6... | collective-permute-start | bytes 393224 | tf_op jit(solution)/shard_map/ppermute | solution.py:13
  173.8 14.0 %collective-permute-start.12 = (bf16[128,512]{1,0:T(8,128)(2,1)S(1)}, bf16[128,512]{1,0:T(8,128)(2,1)S(1)}, u32[]{:S(2)}, u32[]{:S(2)}) collective-permute-start(bf16[128,512]{1,0:T(8,128)(2,1)S(1)} %collective-permute-done.11), channel_id=1, source_target_pairs={{0,8},{8,16},{16,24},{24,32},{32,40},{40,48},{48,56},{56,64},{64,7... | collective-permute-start | bytes 393224 | tf_op jit(solution)/shard_map/ppermute | solution.py:13
  176.2 21.9 %collective-permute-start.4 = (bf16[128,512]{1,0:T(8,128)(2,1)S(1)}, bf16[128,512]{1,0:T(8,128)(2,1)S(1)}, u32[]{:S(2)}, u32[]{:S(2)}) collective-permute-start(bf16[128,512]{1,0:T(8,128)(2,1)S(1)} %collective-permute-done.3), channel_id=1, source_target_pairs={{8,0},{16,8},{24,16},{32,24},{40,32},{48,40},{56,48},{64,56},{72,6... | collective-permute-start | bytes 393224 | tf_op jit(solution)/shard_map/ppermute | solution.py:13
  187.8 26.0 %collective-permute-start.13 = (bf16[128,512]{1,0:T(8,128)(2,1)S(1)}, bf16[128,512]{1,0:T(8,128)(2,1)S(1)}, u32[]{:S(2)}, u32[]{:S(2)}) collective-permute-start(bf16[128,512]{1,0:T(8,128)(2,1)S(1)} %collective-permute-done.12), channel_id=1, source_target_pairs={{0,8},{8,16},{16,24},{24,32},{32,40},{40,48},{48,56},{56,64},{64,7... | collective-permute-start | bytes 393224 | tf_op jit(solution)/shard_map/ppermute | solution.py:13
  198.1 17.6 %collective-permute-start.5 = (bf16[128,512]{1,0:T(8,128)(2,1)S(1)}, bf16[128,512]{1,0:T(8,128)(2,1)S(1)}, u32[]{:S(2)}, u32[]{:S(2)}) collective-permute-start(bf16[128,512]{1,0:T(8,128)(2,1)S(1)} %collective-permute-done.4), channel_id=1, source_target_pairs={{8,0},{16,8},{24,16},{32,24},{40,32},{48,40},{56,48},{64,56},{72,6... | collective-permute-start | bytes 393224 | tf_op jit(solution)/shard_map/ppermute | solution.py:13
  213.8 13.8 %collective-permute-start.14 = (bf16[128,512]{1,0:T(8,128)(2,1)S(1)}, bf16[128,512]{1,0:T(8,128)(2,1)S(1)}, u32[]{:S(2)}, u32[]{:S(2)}) collective-permute-start(bf16[128,512]{1,0:T(8,128)(2,1)S(1)} %collective-permute-done.13), channel_id=1, source_target_pairs={{0,8},{8,16},{16,24},{24,32},{32,40},{40,48},{48,56},{56,64},{64,7... | collective-permute-start | bytes 393224 | tf_op jit(solution)/shard_map/ppermute | solution.py:13
  215.7 13.8 %collective-permute-start.6 = (bf16[128,512]{1,0:T(8,128)(2,1)S(1)}, bf16[128,512]{1,0:T(8,128)(2,1)S(1)}, u32[]{:S(2)}, u32[]{:S(2)}) collective-permute-start(bf16[128,512]{1,0:T(8,128)(2,1)S(1)} %collective-permute-done.5), channel_id=1, source_target_pairs={{8,0},{16,8},{24,16},{32,24},{40,32},{48,40},{56,48},{64,56},{72,6... | collective-permute-start | bytes 393224 | tf_op jit(solution)/shard_map/ppermute | solution.py:13
  227.6 18.0 %collective-permute-start.15 = (bf16[128,512]{1,0:T(8,128)(2,1)S(1)}, bf16[128,512]{1,0:T(8,128)(2,1)S(1)}, u32[]{:S(2)}, u32[]{:S(2)}) collective-permute-start(bf16[128,512]{1,0:T(8,128)(2,1)S(1)} %collective-permute-done.14), channel_id=1, source_target_pairs={{0,8},{8,16},{16,24},{24,32},{32,40},{40,48},{48,56},{56,64},{64,7... | collective-permute-start | bytes 393224 | tf_op jit(solution)/shard_map/ppermute | solution.py:13
  229.5 13.7 %collective-permute-start.7 = (bf16[128,512]{1,0:T(8,128)(2,1)S(1)}, bf16[128,512]{1,0:T(8,128)(2,1)S(1)}, u32[]{:S(2)}, u32[]{:S(2)}) collective-permute-start(bf16[128,512]{1,0:T(8,128)(2,1)S(1)} %collective-permute-done.6), channel_id=1, source_target_pairs={{8,0},{16,8},{24,16},{32,24},{40,32},{48,40},{56,48},{64,56},{72,6... | collective-permute-start | bytes 393224 | tf_op jit(solution)/shard_map/ppermute | solution.py:13
  258.3 549.7 %reduce-scatter.7.cloned.1.call-start = ((), (), s32[]{:S(2)}) async-start(), calls=%async_computation.4 | async-start | bytes 294912
  267.6 8.1 copy-start.2
  267.6 8.1 copy-start.3
  267.6 9.5 %copy-start.4 = (bf16[128,512]{1,0:T(8,128)(2,1)S(1)}, bf16[128,512]{1,0:T(8,128)(2,1)}, u32[]{:S(2)}) copy-start(bf16[128,512]{1,0:T(8,128)(2,1)} %param.5) | copy-start | bytes 393220
  267.6 9.5 %copy-start.5 = (bf16[128,512]{1,0:T(8,128)(2,1)S(1)}, bf16[128,512]{1,0:T(8,128)(2,1)}, u32[]{:S(2)}) copy-start(bf16[128,512]{1,0:T(8,128)(2,1)} %param.7) | copy-start | bytes 393220
  275.7 392.7 %copy-start.6 = (bf16[128,512]{1,0:T(8,128)(2,1)S(1)}, bf16[128,512]{1,0:T(8,128)(2,1)}, u32[]{:S(2)}) copy-start(bf16[128,512]{1,0:T(8,128)(2,1)} %param.8) | copy-start | bytes 393220
  (2 other events, 4.7 us)
Sparse Core Ops, SparseCore 0:
  126.8 90.6 all-gather.1
  668.6 139.3 reduce-scatter.6
Sparse Core Ops, SparseCore 1:
  258.4 408.4 reduce-scatter.4
where the time goes:
time: 818 us; the launch traced here: 817 us
  waiting for transfers between devices  545 us (67%)
  blocking collectives  115 us (14%)
  starting transfers between devices  96.9 us (12%)
  matrix products  20.1 us (2%)
  other arithmetic  16.4 us (2%)
  between operations  16 us (2%)
    reduce_scatter x1, waiting for transfers between devices, local(): lax.psum_scatter(filter_terms, 'ctx', scatter_dimension=0, tiled=True)  388 us
    unnamed x4, waiting for transfers between devices  138 us
    all_gather x1, blocking collectives, local(): piece = lax.all_gather(filter_raw, 'ctx', axis=0, tiled=True)  115 us
    ppermute x16, starting transfers between devices, shifted(): return lax.ppermute(value, axis, pairs)  96.6 us
    ppermute x16, waiting for transfers between devices, shifted(): return lax.ppermute(value, axis, pairs)  18.5 us
  transfers between devices with their start and end apart: 19, of which 11 were waited for; matrix products, arithmetic and copies ran while one was open for 5% of the time, Pallas kernels for 0%

commit v1 on v0

--- a/solution.py
+++ b/solution.py
@@ -53,7 +53,10 @@
 def local(x_one, x_two, values, grad_out, filter_raw):
     tok, chans = x_one.shape
     piece = lax.all_gather(filter_raw, "ctx", axis=0, tiled=True)
-    whole = lax.all_gather(piece, "ch", axis=1, tiled=True)
+    count = lax.axis_size("ch")
+    pieces = jnp.stack([piece for _ in range(count)])
+    pieces = lax.all_to_all(pieces, "ch", split_axis=0, concat_axis=0)
+    whole = jnp.concatenate(pieces, axis=1)
     taps, groups = whole.shape
     span = taps // tok
     repeat = chans // groups

time: 818 us -> 849 us (1.038)
  waiting for transfers between devices: 545 us -> 576 us
  starting transfers between devices: 96.9 us -> 108 us
  other arithmetic: 16.4 us -> 7.88 us
    ppermute x16, waiting for transfers between devices: 18.5 us -> 41.3 us  [shifted(): return lax.ppermute(value, axis, pairs)]
    all_to_all x0 -> x1, starting transfers between devices: none -> 10 us  [local(): pieces = lax.all_to_all(pieces, 'ch', split_axis=0, concat_axis=0)]
    unnamed x4 -> x3, waiting for transfers between devices: 138 us -> 142 us
  transfers between devices with their start and end apart: 19 -> 19, of which waited for: 11 -> 11; matrix products, arithmetic and copies ran while one was open for 5% -> 3% of each run, Pallas kernels for 0% -> 0%
where the time goes in v1:
time: 849 us; the launch traced here: 848 us
  waiting for transfers between devices  576 us (68%)
  blocking collectives  115 us (14%)
  starting transfers between devices  108 us (13%)
  matrix products  19.8 us (2%)
  between operations  14.7 us (2%)
    reduce_scatter x1, waiting for transfers between devices, local(): lax.psum_scatter(filter_terms, 'ctx', scatter_dimension=0, tiled=True)  393 us
    unnamed x3, waiting for transfers between devices  142 us
    all_gather x1, blocking collectives, local(): piece = lax.all_gather(filter_raw, 'ctx', axis=0, tiled=True)  115 us
    ppermute x16, starting transfers between devices, shifted(): return lax.ppermute(value, axis, pairs)  97.7 us
    ppermute x16, waiting for transfers between devices, shifted(): return lax.ppermute(value, axis, pairs)  41.3 us
  transfers between devices with their start and end apart: 19, of which 11 were waited for; matrix products, arithmetic and copies ran while one was open for 3% of the time, Pallas kernels for 0%

profile of v1, /device:TPU:8, one launch (start us, length us, event | category | flops | bytes accessed | tf_op | source)
XLA Modules:
  0.0 847.7 jit_solution(11972497359706276061)
XLA Ops:
  8.2 1.9 collective-permute-start.8
  10.2 114.8 %all_gather.3 = bf16[1024,64]{1,0:T(8,128)(2,1)S(1)} all-gather(bf16[16,64]{1,0:T(8,128)(2,1)} %param.9), channel_id=1, replica_groups=mesh['ctx'=64,'ch'=8] {'ctx'}, dimensions={0}, use_global_device_ids=true | all-gather | bytes 133120 | tf_op jit(solution)/shard_map/all_gather | solution.py:55
  126.2 10.0 %all-to-all-start = ((bf16[8,1024,64]{1,2,0:T(8,128)(2,1)}), bf16[8,1024,64]{1,2,0:T(8,128)(2,1)S(1)}, u32[]{:S(2)}, u32[]{:S(2)}) async-start(bf16[8,1024,64]{1,2,0:T(8,128)(2,1)} %stack.71), calls=%async_computation | async-start | bytes 2097152 | tf_op jit(solution)/shard_map/all_to_all | solution.py:58
  136.4 1.9 collective-permute-start
  139.5 2.4 collective-permute-start.9
  141.9 35.8 %collective-permute-done = bf16[128,512]{1,0:T(8,128)(2,1)S(1)} collective-permute-done((bf16[128,512]{1,0:T(8,128)(2,1)S(1)}, bf16[128,512]{1,0:T(8,128)(2,1)S(1)}, u32[]{:S(2)}, u32[]{:S(2)}) %collective-permute-start) | collective-permute-done | bytes 131104 | tf_op jit(solution)/shard_map/ppermute | solution.py:13
  177.8 11.4 %collective-permute-start.1 = (bf16[128,512]{1,0:T(8,128)(2,1)S(1)}, bf16[128,512]{1,0:T(8,128)(2,1)S(1)}, u32[]{:S(2)}, u32[]{:S(2)}) collective-permute-start(bf16[128,512]{1,0:T(8,128)(2,1)S(1)} %collective-permute-done), channel_id=1, source_target_pairs={{8,0},{16,8},{24,16},{32,24},{40,32},{48,40},{56,48},{64,56},{72,6... | collective-permute-start | bytes 393224 | tf_op jit(solution)/shard_map/ppermute | solution.py:13
  191.7 11.4 %collective-permute-start.2 = (bf16[128,512]{1,0:T(8,128)(2,1)S(1)}, bf16[128,512]{1,0:T(8,128)(2,1)S(1)}, u32[]{:S(2)}, u32[]{:S(2)}) collective-permute-start(bf16[128,512]{1,0:T(8,128)(2,1)S(1)} %collective-permute-done.1), channel_id=1, source_target_pairs={{8,0},{16,8},{24,16},{32,24},{40,32},{48,40},{56,48},{64,56},{72,6... | collective-permute-start | bytes 393224 | tf_op jit(solution)/shard_map/ppermute | solution.py:13
  203.1 1.9 collective-permute-start.11
  205.6 11.5 %collective-permute-start.3 = (bf16[128,512]{1,0:T(8,128)(2,1)S(1)}, bf16[128,512]{1,0:T(8,128)(2,1)S(1)}, u32[]{:S(2)}, u32[]{:S(2)}) collective-permute-start(bf16[128,512]{1,0:T(8,128)(2,1)S(1)} %collective-permute-done.2), channel_id=1, source_target_pairs={{8,0},{16,8},{24,16},{32,24},{40,32},{48,40},{56,48},{64,56},{72,6... | collective-permute-start | bytes 393224 | tf_op jit(solution)/shard_map/ppermute | solution.py:13
  217.2 1.9 collective-permute-start.12
  219.6 11.4 %collective-permute-start.4 = (bf16[128,512]{1,0:T(8,128)(2,1)S(1)}, bf16[128,512]{1,0:T(8,128)(2,1)S(1)}, u32[]{:S(2)}, u32[]{:S(2)}) collective-permute-start(bf16[128,512]{1,0:T(8,128)(2,1)S(1)} %collective-permute-done.3), channel_id=1, source_target_pairs={{8,0},{16,8},{24,16},{32,24},{40,32},{48,40},{56,48},{64,56},{72,6... | collective-permute-start | bytes 393224 | tf_op jit(solution)/shard_map/ppermute | solution.py:13
  233.5 11.4 %collective-permute-start.5 = (bf16[128,512]{1,0:T(8,128)(2,1)S(1)}, bf16[128,512]{1,0:T(8,128)(2,1)S(1)}, u32[]{:S(2)}, u32[]{:S(2)}) collective-permute-start(bf16[128,512]{1,0:T(8,128)(2,1)S(1)} %collective-permute-done.4), channel_id=1, source_target_pairs={{8,0},{16,8},{24,16},{32,24},{40,32},{48,40},{56,48},{64,56},{72,6... | collective-permute-start | bytes 393224 | tf_op jit(solution)/shard_map/ppermute | solution.py:13
  244.9 1.9 collective-permute-start.14
  247.4 11.4 %collective-permute-start.6 = (bf16[128,512]{1,0:T(8,128)(2,1)S(1)}, bf16[128,512]{1,0:T(8,128)(2,1)S(1)}, u32[]{:S(2)}, u32[]{:S(2)}) collective-permute-start(bf16[128,512]{1,0:T(8,128)(2,1)S(1)} %collective-permute-done.5), channel_id=1, source_target_pairs={{8,0},{16,8},{24,16},{32,24},{40,32},{48,40},{56,48},{64,56},{72,6... | collective-permute-start | bytes 393224 | tf_op jit(solution)/shard_map/ppermute | solution.py:13
  261.3 11.5 %collective-permute-start.7 = (bf16[128,512]{1,0:T(8,128)(2,1)S(1)}, bf16[128,512]{1,0:T(8,128)(2,1)S(1)}, u32[]{:S(2)}, u32[]{:S(2)}) collective-permute-start(bf16[128,512]{1,0:T(8,128)(2,1)S(1)} %collective-permute-done.6), channel_id=1, source_target_pairs={{8,0},{16,8},{24,16},{32,24},{40,32},{48,40},{56,48},{64,56},{72,6... | collective-permute-start | bytes 393224 | tf_op jit(solution)/shard_map/ppermute | solution.py:13
  272.8 2.3 collective-permute-done.7
  275.1 2.3 convolution_bitcast_fusion.1
  277.5 2.4 convolution_bitcast_fusion
  283.3 7.3 fusion.7
  291.6 3.8 convolution_bitcast_fusion.2
  295.5 3.6 subtract_reduce_fusion
  301.9 392.9 %reduce-scatter.5.cloned.1.call-done = f32[16,512]{1,0:T(8,128)} async-done(((f32[1024,512]{1,0:T(8,128)}), f32[16,512]{1,0:T(8,128)}) %reduce-scatter.5.cloned.1.call-update) | async-done | bytes 32784 | tf_op jit(solution)/shard_map/reduce_scatter | solution.py:119
  697.7 141.8 %reduce-scatter.7.cloned.1.call-done = f32[64,16]{1,0:T(8,128)} async-done(((f32[512,16]{1,0:T(8,128)}), f32[64,16]{1,0:T(8,128)}) %reduce-scatter.7.cloned.1.call-update) | async-done | bytes 4112
  (80 shorter events, 24.1 us)
Async XLA Ops:
  7.2 129.2 %copy-start.5 = (bf16[128,512]{1,0:T(8,128)(2,1)S(1)}, bf16[128,512]{1,0:T(8,128)(2,1)}, u32[]{:S(2)}) copy-start(bf16[128,512]{1,0:T(8,128)(2,1)} %param.6) | copy-start | bytes 393220
  7.2 129.2 %copy-start.4 = (bf16[128,512]{1,0:T(8,128)(2,1)S(1)}, bf16[128,512]{1,0:T(8,128)(2,1)}, u32[]{:S(2)}) copy-start(bf16[128,512]{1,0:T(8,128)(2,1)} %param.8) | copy-start | bytes 393220
  8.2 131.3 %collective-permute-start.8 = (bf16[128,512]{1,0:T(8,128)(2,1)S(1)}, bf16[128,512]{1,0:T(8,128)(2,1)S(1)}, u32[]{:S(2)}, u32[]{:S(2)}) collective-permute-start(bf16[128,512]{1,0:T(8,128)(2,1)S(1)} %get-tuple-element.13), channel_id=1, source_target_pairs={{0,8},{8,16},{16,24},{24,32},{32,40},{40,48},{48,56},{56,64},{64,7... | collective-permute-start | bytes 393224 | tf_op jit(solution)/shard_map/ppermute | solution.py:13
  126.2 164.6 %all-to-all-start = ((bf16[8,1024,64]{1,2,0:T(8,128)(2,1)}), bf16[8,1024,64]{1,2,0:T(8,128)(2,1)S(1)}, u32[]{:S(2)}, u32[]{:S(2)}) async-start(bf16[8,1024,64]{1,2,0:T(8,128)(2,1)} %stack.71), calls=%async_computation | async-start | bytes 2097152 | tf_op jit(solution)/shard_map/all_to_all | solution.py:58
  136.3 558.5 %reduce-scatter.5.cloned.1.call-start = ((), (), s32[]{:S(2)}) async-start(), calls=%async_computation.3 | async-start | bytes 2129920 | tf_op jit(solution)/shard_map/reduce_scatter | solution.py:119
  136.4 41.4 %collective-permute-start = (bf16[128,512]{1,0:T(8,128)(2,1)S(1)}, bf16[128,512]{1,0:T(8,128)(2,1)S(1)}, u32[]{:S(2)}, u32[]{:S(2)}) collective-permute-start(bf16[128,512]{1,0:T(8,128)(2,1)S(1)} %get-tuple-element.15), channel_id=1, source_target_pairs={{8,0},{16,8},{24,16},{32,24},{40,32},{48,40},{56,48},{64,56},{72,6... | collective-permute-start | bytes 393224 | tf_op jit(solution)/shard_map/ppermute | solution.py:13
  139.5 49.7 %collective-permute-start.9 = (bf16[128,512]{1,0:T(8,128)(2,1)S(1)}, bf16[128,512]{1,0:T(8,128)(2,1)S(1)}, u32[]{:S(2)}, u32[]{:S(2)}) collective-permute-start(bf16[128,512]{1,0:T(8,128)(2,1)S(1)} %collective-permute-done.8), channel_id=1, source_target_pairs={{0,8},{8,16},{16,24},{24,32},{32,40},{40,48},{48,56},{56,64},{64,7... | collective-permute-start | bytes 393224 | tf_op jit(solution)/shard_map/ppermute | solution.py:13
  177.8 13.9 %collective-permute-start.1 = (bf16[128,512]{1,0:T(8,128)(2,1)S(1)}, bf16[128,512]{1,0:T(8,128)(2,1)S(1)}, u32[]{:S(2)}, u32[]{:S(2)}) collective-permute-start(bf16[128,512]{1,0:T(8,128)(2,1)S(1)} %collective-permute-done), channel_id=1, source_target_pairs={{8,0},{16,8},{24,16},{32,24},{40,32},{48,40},{56,48},{64,56},{72,6... | collective-permute-start | bytes 393224 | tf_op jit(solution)/shard_map/ppermute | solution.py:13
  189.2 13.9 %collective-permute-start.10 = (bf16[128,512]{1,0:T(8,128)(2,1)S(1)}, bf16[128,512]{1,0:T(8,128)(2,1)S(1)}, u32[]{:S(2)}, u32[]{:S(2)}) collective-permute-start(bf16[128,512]{1,0:T(8,128)(2,1)S(1)} %collective-permute-done.9), channel_id=1, source_target_pairs={{0,8},{8,16},{16,24},{24,32},{32,40},{40,48},{48,56},{56,64},{64,7... | collective-permute-start | bytes 393224 | tf_op jit(solution)/shard_map/ppermute | solution.py:13
  191.7 13.9 %collective-permute-start.2 = (bf16[128,512]{1,0:T(8,128)(2,1)S(1)}, bf16[128,512]{1,0:T(8,128)(2,1)S(1)}, u32[]{:S(2)}, u32[]{:S(2)}) collective-permute-start(bf16[128,512]{1,0:T(8,128)(2,1)S(1)} %collective-permute-done.1), channel_id=1, source_target_pairs={{8,0},{16,8},{24,16},{32,24},{40,32},{48,40},{56,48},{64,56},{72,6... | collective-permute-start | bytes 393224 | tf_op jit(solution)/shard_map/ppermute | solution.py:13
  203.1 14.0 %collective-permute-start.11 = (bf16[128,512]{1,0:T(8,128)(2,1)S(1)}, bf16[128,512]{1,0:T(8,128)(2,1)S(1)}, u32[]{:S(2)}, u32[]{:S(2)}) collective-permute-start(bf16[128,512]{1,0:T(8,128)(2,1)S(1)} %collective-permute-done.10), channel_id=1, source_target_pairs={{0,8},{8,16},{16,24},{24,32},{32,40},{40,48},{48,56},{56,64},{64,7... | collective-permute-start | bytes 393224 | tf_op jit(solution)/shard_map/ppermute | solution.py:13
  205.6 14.0 %collective-permute-start.3 = (bf16[128,512]{1,0:T(8,128)(2,1)S(1)}, bf16[128,512]{1,0:T(8,128)(2,1)S(1)}, u32[]{:S(2)}, u32[]{:S(2)}) collective-permute-start(bf16[128,512]{1,0:T(8,128)(2,1)S(1)} %collective-permute-done.2), channel_id=1, source_target_pairs={{8,0},{16,8},{24,16},{32,24},{40,32},{48,40},{56,48},{64,56},{72,6... | collective-permute-start | bytes 393224 | tf_op jit(solution)/shard_map/ppermute | solution.py:13
  217.2 14.0 %collective-permute-start.12 = (bf16[128,512]{1,0:T(8,128)(2,1)S(1)}, bf16[128,512]{1,0:T(8,128)(2,1)S(1)}, u32[]{:S(2)}, u32[]{:S(2)}) collective-permute-start(bf16[128,512]{1,0:T(8,128)(2,1)S(1)} %collective-permute-done.11), channel_id=1, source_target_pairs={{0,8},{8,16},{16,24},{24,32},{32,40},{40,48},{48,56},{56,64},{64,7... | collective-permute-start | bytes 393224 | tf_op jit(solution)/shard_map/ppermute | solution.py:13
  219.6 13.9 %collective-permute-start.4 = (bf16[128,512]{1,0:T(8,128)(2,1)S(1)}, bf16[128,512]{1,0:T(8,128)(2,1)S(1)}, u32[]{:S(2)}, u32[]{:S(2)}) collective-permute-start(bf16[128,512]{1,0:T(8,128)(2,1)S(1)} %collective-permute-done.3), channel_id=1, source_target_pairs={{8,0},{16,8},{24,16},{32,24},{40,32},{48,40},{56,48},{64,56},{72,6... | collective-permute-start | bytes 393224 | tf_op jit(solution)/shard_map/ppermute | solution.py:13
  231.1 13.8 %collective-permute-start.13 = (bf16[128,512]{1,0:T(8,128)(2,1)S(1)}, bf16[128,512]{1,0:T(8,128)(2,1)S(1)}, u32[]{:S(2)}, u32[]{:S(2)}) collective-permute-start(bf16[128,512]{1,0:T(8,128)(2,1)S(1)} %collective-permute-done.12), channel_id=1, source_target_pairs={{0,8},{8,16},{16,24},{24,32},{32,40},{40,48},{48,56},{56,64},{64,7... | collective-permute-start | bytes 393224 | tf_op jit(solution)/shard_map/ppermute | solution.py:13
  233.5 13.9 %collective-permute-start.5 = (bf16[128,512]{1,0:T(8,128)(2,1)S(1)}, bf16[128,512]{1,0:T(8,128)(2,1)S(1)}, u32[]{:S(2)}, u32[]{:S(2)}) collective-permute-start(bf16[128,512]{1,0:T(8,128)(2,1)S(1)} %collective-permute-done.4), channel_id=1, source_target_pairs={{8,0},{16,8},{24,16},{32,24},{40,32},{48,40},{56,48},{64,56},{72,6... | collective-permute-start | bytes 393224 | tf_op jit(solution)/shard_map/ppermute | solution.py:13
  244.9 13.9 %collective-permute-start.14 = (bf16[128,512]{1,0:T(8,128)(2,1)S(1)}, bf16[128,512]{1,0:T(8,128)(2,1)S(1)}, u32[]{:S(2)}, u32[]{:S(2)}) collective-permute-start(bf16[128,512]{1,0:T(8,128)(2,1)S(1)} %collective-permute-done.13), channel_id=1, source_target_pairs={{0,8},{8,16},{16,24},{24,32},{32,40},{40,48},{48,56},{56,64},{64,7... | collective-permute-start | bytes 393224 | tf_op jit(solution)/shard_map/ppermute | solution.py:13
  247.4 13.9 %collective-permute-start.6 = (bf16[128,512]{1,0:T(8,128)(2,1)S(1)}, bf16[128,512]{1,0:T(8,128)(2,1)S(1)}, u32[]{:S(2)}, u32[]{:S(2)}) collective-permute-start(bf16[128,512]{1,0:T(8,128)(2,1)S(1)} %collective-permute-done.5), channel_id=1, source_target_pairs={{8,0},{16,8},{24,16},{32,24},{40,32},{48,40},{56,48},{64,56},{72,6... | collective-permute-start | bytes 393224 | tf_op jit(solution)/shard_map/ppermute | solution.py:13
  258.8 18.7 %collective-permute-start.15 = (bf16[128,512]{1,0:T(8,128)(2,1)S(1)}, bf16[128,512]{1,0:T(8,128)(2,1)S(1)}, u32[]{:S(2)}, u32[]{:S(2)}) collective-permute-start(bf16[128,512]{1,0:T(8,128)(2,1)S(1)} %collective-permute-done.14), channel_id=1, source_target_pairs={{0,8},{8,16},{16,24},{24,32},{32,40},{40,48},{48,56},{56,64},{64,7... | collective-permute-start | bytes 393224 | tf_op jit(solution)/shard_map/ppermute | solution.py:13
  261.3 13.8 %collective-permute-start.7 = (bf16[128,512]{1,0:T(8,128)(2,1)S(1)}, bf16[128,512]{1,0:T(8,128)(2,1)S(1)}, u32[]{:S(2)}, u32[]{:S(2)}) collective-permute-start(bf16[128,512]{1,0:T(8,128)(2,1)S(1)} %collective-permute-done.6), channel_id=1, source_target_pairs={{8,0},{16,8},{24,16},{32,24},{40,32},{48,40},{56,48},{64,56},{72,6... | collective-permute-start | bytes 393224 | tf_op jit(solution)/shard_map/ppermute | solution.py:13
  290.5 548.9 %reduce-scatter.7.cloned.1.call-start = ((), (), s32[]{:S(2)}) async-start(), calls=%async_computation.4 | async-start | bytes 294912
  290.8 4.6 slice-start
  295.5 5.0 copy-start.2
  295.5 5.0 copy-start.3
  (5 other events, 18.2 us)
Sparse Core Ops, SparseCore 0:
  290.7 404.0 reduce-scatter.4
  699.8 139.5 reduce-scatter.6
